TPU v7x, 256 devices: a whole 4x4x8 slice. The times are simulated.
256 devices in a mesh: dp: 16 (over z, x_lo), tensor: 16 (over y, x_hi, core).
Axes of the slice: x: 4 (x_hi: 2, x_lo: 2; x = x_hi * 2 + x_lo), y: 4, z: 8, core: 2. Of those that a mesh axis runs over, the one named last changes fastest.
Arguments:
- gate_act: bfloat16 [2048, 26624], P('dp', 'tensor'), may hold values from -8 to 8
- up_act: bfloat16 [2048, 26624], P('dp', 'tensor'), may hold values from -6 to 6
- down_codes: bfloat16 [26624, 16384], P('tensor', 'dp'), may hold values from -4 to 4
- down_scales: float32 [208, 128], P('tensor', 'dp'), may hold values from 0.0024514517 to 0.024514517
- grad_out: bfloat16 [2048, 16384], P('tensor', 'dp'), may hold values from -6 to 6
Outputs:
- layer_output: bfloat16 [2048, 16384], P('tensor', 'dp')
- gate_grad: bfloat16 [2048, 26624], P('dp', 'tensor')
- up_grad: bfloat16 [2048, 26624], P('dp', 'tensor')
All inputs are finite; a program needn't handle non-finite values.
Results may differ from a plain program's by a relative error of at most 0.027.
Values may be sent and summed in bfloat16 or wider, within the bound.
A program may use at most 128 MiB of HBM per device.

v0:
```python
import math

import jax
import jax.numpy as jnp
from jax import lax
from jax.sharding import PartitionSpec as P

BLOCK = 128


def from_partner(value, axis, stride):
    return lax.ppermute(value, axis, [(i, i ^ 1 << stride) for i in range(lax.axis_size(axis))])


def sylvester(matrix_order):
    indices = jnp.arange(matrix_order, dtype=jnp.int32)
    common_bits = indices[:, None] & indices[None, :]
    parity = jnp.zeros((matrix_order, matrix_order), jnp.int32)
    for section_bit in range(max(matrix_order.bit_length() - 1, 0)):
        parity = parity + (common_bits >> section_bit & 1)
    return (1 - 2 * (parity % 2)).astype(jnp.float32)


def dequantize(code_block, scale_block):
    row_count, col_count = code_block.shape
    expanded = code_block.astype(jnp.float32).reshape(
        row_count // BLOCK, BLOCK, col_count // BLOCK, BLOCK
    )
    return (
        (expanded * scale_block[:, None, :, None])
        .reshape(row_count, col_count)
        .astype(jnp.bfloat16)
    )


def local_mix(values, group_size):
    row_count, col_count = values.shape
    shaped = values.reshape(row_count, col_count // BLOCK, BLOCK)
    mixed_values = jnp.einsum(
        "rbc,dc->rbd", shaped, sylvester(BLOCK), precision=lax.Precision.HIGHEST
    )
    return (mixed_values / math.sqrt(group_size * BLOCK)).reshape(row_count, col_count)


def rotate_pairs(values):
    group_size = lax.axis_size("tensor")
    position = lax.axis_index("tensor")
    current = values.astype(jnp.float32)
    for section_bit in range(group_size.bit_length() - 1):
        partner = from_partner(current.astype(jnp.bfloat16), "tensor", section_bit).astype(
            current.dtype
        )
        upper_half = position >> section_bit & 1 == 1
        current = jnp.where(upper_half, partner - current, current + partner)
    return local_mix(current, group_size).astype(jnp.bfloat16)


def rotate(values):
    return rotate_pairs(values)


def on_device(gate_act, up_act, down_codes, down_scales, grad_out):
    gate_wide = gate_act.astype(jnp.float32)
    up_wide = up_act.astype(jnp.float32)
    sigmoid_gate = jax.nn.sigmoid(gate_wide)
    silu_gate = gate_wide * sigmoid_gate
    hidden = (silu_gate * up_wide).astype(jnp.bfloat16)
    rotated = rotate(hidden)
    weight = dequantize(down_codes, down_scales)
    partial_value = jnp.dot(
        lax.all_gather(rotated, "dp", axis=0, tiled=True),
        weight,
        preferred_element_type=jnp.float32,
    )
    layer_output = lax.psum_scatter(
        partial_value.astype(jnp.bfloat16), "tensor", scatter_dimension=0, tiled=True
    )
    grad_rows = lax.all_gather(grad_out, "tensor", axis=0, tiled=True)
    grad_rotated = lax.psum_scatter(
        lax.dot_general(
            grad_rows, weight, (((1,), (1,)), ((), ())), preferred_element_type=jnp.float32
        ).astype(jnp.bfloat16),
        "dp",
        scatter_dimension=0,
        tiled=True,
    )
    grad_hidden = rotate(grad_rotated).astype(jnp.float32)
    up_grad = (grad_hidden * silu_gate).astype(jnp.bfloat16)
    gate_grad = (
        grad_hidden * up_wide * sigmoid_gate * (1.0 + gate_wide * (1.0 - sigmoid_gate))
    ).astype(jnp.bfloat16)
    return (layer_output, gate_grad, up_grad)


def solution(mesh):
    return jax.shard_map(
        on_device,
        mesh=mesh,
        in_specs=(
            P("dp", "tensor"),
            P("dp", "tensor"),
            P("tensor", "dp"),
            P("tensor", "dp"),
            P("tensor", "dp"),
        ),
        out_specs=(P("tensor", "dp"), P("dp", "tensor"), P("dp", "tensor")),
        check_vma=False,
    )
```

profile of v0, /device:TPU:1, one launch (start us, length us, event | category | flops | bytes accessed | tf_op | source)
XLA Modules:
  0.0 614.8 jit_solution(7300220002962055497)
XLA Ops:
  8.7 66.6 %all-gather.5.cloned.1.call-done = bf16[2048,1024]{1,0:T(8,128)(2,1)} async-done(((bf16[128,1024]{1,0:T(8,128)(2,1)}), bf16[2048,1024]{1,0:T(8,128)(2,1)}) %all-gather.5.cloned.1.call-update) | async-done | bytes 4194320 | tf_op jit(solution)/shard_map/all_gather | solution.py:78
  75.9 3.1 copy-done
  79.3 11.5 %fusion.1 = bf16[2048,1664]{0,1:T(8,128)(2,1)} fusion(bf16[2048,1024]{1,0:T(8,128)(2,1)S(1)} %copy-done.3, f32[208,8,8,128]{3,2,1,0:T(8,128)S(1)} %bitcast.26, bf16[1664,1024]{1,0:T(8,128)(2,1)} %param.7), kind=kOutput, calls=%fused_computation.3 | convolution fusion | flops 6987841536 | bytes 21233664 | tf_op jit(solution)/shard_map/dot_general | solution.py:80
  90.9 9.7 %copy.24 = bf16[2048,1664]{1,0:T(8,128)(2,1)} copy(bf16[2048,1664]{0,1:T(8,128)(2,1)} %fusion.1) | data formatting | bytes 13631488
  100.7 148.2 %reduce-scatter.7.cloned.1.call-done = bf16[128,1664]{1,0:T(8,128)(2,1)} async-done(((bf16[2048,1664]{1,0:T(8,128)(2,1)}), bf16[128,1664]{1,0:T(8,128)(2,1)}) %reduce-scatter.7.cloned.1.call-update) | async-done | bytes 426000
  251.5 1.4 collective-permute-done.4
  253.1 3.0 collective-permute-start.5
  256.1 9.6 %collective-permute-done.5 = bf16[128,1664]{0,1:T(8,128)(2,1)S(1)} collective-permute-done((bf16[128,1664]{0,1:T(8,128)(2,1)S(1)}, bf16[128,1664]{0,1:T(8,128)(2,1)S(1)}, u32[]{:S(2)}, u32[]{:S(2)}) %collective-permute-start.5) | collective-permute-done | bytes 426016 | tf_op jit(solution)/shard_map/ppermute | solution.py:12
  266.0 1.5 collective-permute-start.6
  267.5 8.7 %collective-permute-done.6 = bf16[128,1664]{0,1:T(8,128)(2,1)S(1)} collective-permute-done((bf16[128,1664]{0,1:T(8,128)(2,1)S(1)}, bf16[128,1664]{0,1:T(8,128)(2,1)S(1)}, u32[]{:S(2)}, u32[]{:S(2)}) %collective-permute-start.6) | collective-permute-done | bytes 426016 | tf_op jit(solution)/shard_map/ppermute | solution.py:12
  277.3 2.9 collective-permute-start.7
  280.8 7.4 %collective-permute-done.7 = bf16[128,1664]{0,1:T(8,128)(2,1)S(1)} collective-permute-done((bf16[128,1664]{0,1:T(8,128)(2,1)}, bf16[128,1664]{0,1:T(8,128)(2,1)S(1)}, u32[]{:S(2)}, u32[]{:S(2)}) %collective-permute-start.7) | collective-permute-done | bytes 426016 | tf_op jit(solution)/shard_map/ppermute | solution.py:12
  290.2 3.1 collective-permute-start
  293.3 1.4 collective-permute-done
  294.9 3.2 collective-permute-start.1
  298.1 9.6 %collective-permute-done.1 = bf16[128,1664]{0,1:T(8,128)(2,1)S(1)} collective-permute-done((bf16[128,1664]{0,1:T(8,128)(2,1)S(1)}, bf16[128,1664]{0,1:T(8,128)(2,1)S(1)}, u32[]{:S(2)}, u32[]{:S(2)}) %collective-permute-start.1) | collective-permute-done | bytes 426016 | tf_op jit(solution)/shard_map/ppermute | solution.py:12
  308.0 1.5 collective-permute-start.2
  309.5 8.7 %collective-permute-done.2 = bf16[128,1664]{0,1:T(8,128)(2,1)S(1)} collective-permute-done((bf16[128,1664]{0,1:T(8,128)(2,1)S(1)}, bf16[128,1664]{0,1:T(8,128)(2,1)S(1)}, u32[]{:S(2)}, u32[]{:S(2)}) %collective-permute-start.2) | collective-permute-done | bytes 426016 | tf_op jit(solution)/shard_map/ppermute | solution.py:12
  318.6 3.0 collective-permute-start.3
  321.6 7.7 %collective-permute-done.3 = bf16[128,1664]{0,1:T(8,128)(2,1)S(1)} collective-permute-done((bf16[128,1664]{0,1:T(8,128)(2,1)S(1)}, bf16[128,1664]{0,1:T(8,128)(2,1)S(1)}, u32[]{:S(2)}, u32[]{:S(2)}) %collective-permute-start.3) | collective-permute-done | bytes 426016 | tf_op jit(solution)/shard_map/ppermute | solution.py:12
  329.8 1.7 fusion.2
  331.6 164.6 %all-gather.3.cloned.1.call-done = bf16[2048,1664]{0,1:T(8,128)(2,1)} async-done(((bf16[128,1664]{0,1:T(8,128)(2,1)}), bf16[2048,1664]{0,1:T(8,128)(2,1)}) %all-gather.3.cloned.1.call-update) | async-done | bytes 6815760 | tf_op jit(solution)/shard_map/all_gather | solution.py:71
  496.2 14.7 %convolution_convert_fusion.1 = bf16[2048,1024]{1,0:T(8,128)(2,1)} fusion(bf16[2048,1664]{0,1:T(8,128)(2,1)} %all-gather.3.cloned.1.call-done, f32[208,8,8,128]{3,2,1,0:T(8,128)} %bitcast.27, bf16[1664,1024]{1,0:T(8,128)(2,1)} %param.7), kind=kOutput, calls=%fused_computation.4 | convolution fusion | flops 6986530816 | bytes 21233664 | tf_op jit(solution)/shard_map/dot_general | solution.py:70
  512.9 95.3 %reduce-scatter.5.cloned.1.call-done = bf16[128,1024]{1,0:T(8,128)(2,1)} async-done(((bf16[2048,1024]{1,0:T(8,128)(2,1)}), bf16[128,1024]{1,0:T(8,128)(2,1)}) %reduce-scatter.5.cloned.1.call-update) | async-done | bytes 262160 | tf_op jit(solution)/shard_map/reduce_scatter | solution.py:75
  (33 shorter events, 12.5 us)
Async XLA Ops:
  7.2 68.2 %all-gather.5.cloned.1.call-start = ((), (), s32[]{:S(2)}) async-start(), calls=%async_computation.4 | async-start | bytes 4456448 | tf_op jit(solution)/shard_map/all_gather | solution.py:78
  7.9 241.0 %reduce-scatter.7.cloned.1.call-start = ((), (), s32[]{:S(2)}) async-start(), calls=%async_computation.5 | async-start | bytes 7241728
  75.3 4.0 copy-start.3
  75.8 3.2 copy-start
  100.6 179.7 %copy-start.1 = (bf16[128,1664]{1,0:T(8,128)(2,1)S(1)}, bf16[128,1664]{1,0:T(8,128)(2,1)}, u32[]{:S(2)}) copy-start(bf16[128,1664]{1,0:T(8,128)(2,1)} %param.5) | copy-start | bytes 1277956
  100.6 179.9 %copy-start.2 = (bf16[128,1664]{1,0:T(8,128)(2,1)S(1)}, bf16[128,1664]{1,0:T(8,128)(2,1)}, u32[]{:S(2)}) copy-start(bf16[128,1664]{1,0:T(8,128)(2,1)} %param.6) | copy-start | bytes 1277956
  100.6 395.6 %all-gather.3.cloned.1.call-start = ((), (), s32[]{:S(2)}) async-start(), calls=%async_computation.2 | async-start | bytes 7241728 | tf_op jit(solution)/shard_map/all_gather | solution.py:71
  250.1 2.8 collective-permute-start.4
  253.1 12.6 %collective-permute-start.5 = (bf16[128,1664]{0,1:T(8,128)(2,1)S(1)}, bf16[128,1664]{0,1:T(8,128)(2,1)S(1)}, u32[]{:S(2)}, u32[]{:S(2)}) collective-permute-start(bf16[128,1664]{0,1:T(8,128)(2,1)S(1)} %fusion.21), channel_id=1, source_target_pairs={{0,2},{1,3},{2,0},{3,1},{4,6},{5,7},{6,4},{7,5},{8,10},{9,11},{10,... | collective-permute-start | bytes 1277960 | tf_op jit(solution)/shard_map/ppermute | solution.py:12
  266.0 10.2 %collective-permute-start.6 = (bf16[128,1664]{0,1:T(8,128)(2,1)S(1)}, bf16[128,1664]{0,1:T(8,128)(2,1)S(1)}, u32[]{:S(2)}, u32[]{:S(2)}) collective-permute-start(bf16[128,1664]{0,1:T(8,128)(2,1)S(1)} %fusion.60), channel_id=1, source_target_pairs={{0,4},{1,5},{2,6},{3,7},{4,0},{5,1},{6,2},{7,3},{8,12},{9,13},{10,... | collective-permute-start | bytes 1277960 | tf_op jit(solution)/shard_map/ppermute | solution.py:12
  277.3 10.9 %collective-permute-start.7 = (bf16[128,1664]{0,1:T(8,128)(2,1)}, bf16[128,1664]{0,1:T(8,128)(2,1)S(1)}, u32[]{:S(2)}, u32[]{:S(2)}) collective-permute-start(bf16[128,1664]{0,1:T(8,128)(2,1)} %fusion.23), channel_id=1, source_target_pairs={{0,8},{1,9},{2,10},{3,11},{4,12},{5,13},{6,14},{7,15},{8,0},{9,1},... | collective-permute-start | bytes 1277960 | tf_op jit(solution)/shard_map/ppermute | solution.py:12
  290.2 4.5 collective-permute-start
  294.9 12.8 %collective-permute-start.1 = (bf16[128,1664]{0,1:T(8,128)(2,1)S(1)}, bf16[128,1664]{0,1:T(8,128)(2,1)S(1)}, u32[]{:S(2)}, u32[]{:S(2)}) collective-permute-start(bf16[128,1664]{0,1:T(8,128)(2,1)S(1)} %fusion.22), channel_id=1, source_target_pairs={{0,2},{1,3},{2,0},{3,1},{4,6},{5,7},{6,4},{7,5},{8,10},{9,11},{10,... | collective-permute-start | bytes 1277960 | tf_op jit(solution)/shard_map/ppermute | solution.py:12
  308.0 10.2 %collective-permute-start.2 = (bf16[128,1664]{0,1:T(8,128)(2,1)S(1)}, bf16[128,1664]{0,1:T(8,128)(2,1)S(1)}, u32[]{:S(2)}, u32[]{:S(2)}) collective-permute-start(bf16[128,1664]{0,1:T(8,128)(2,1)S(1)} %fusion.61), channel_id=1, source_target_pairs={{0,4},{1,5},{2,6},{3,7},{4,0},{5,1},{6,2},{7,3},{8,12},{9,13},{10,... | collective-permute-start | bytes 1277960 | tf_op jit(solution)/shard_map/ppermute | solution.py:12
  318.6 10.8 %collective-permute-start.3 = (bf16[128,1664]{0,1:T(8,128)(2,1)S(1)}, bf16[128,1664]{0,1:T(8,128)(2,1)S(1)}, u32[]{:S(2)}, u32[]{:S(2)}) collective-permute-start(bf16[128,1664]{0,1:T(8,128)(2,1)S(1)} %fusion.24), channel_id=1, source_target_pairs={{0,8},{1,9},{2,10},{3,11},{4,12},{5,13},{6,14},{7,15},{8,0},{9,1},... | collective-permute-start | bytes 1277960 | tf_op jit(solution)/shard_map/ppermute | solution.py:12
  331.6 276.7 %reduce-scatter.5.cloned.1.call-start = ((), (), s32[]{:S(2)}) async-start(), calls=%async_computation.3 | async-start | bytes 4456448 | tf_op jit(solution)/shard_map/reduce_scatter | solution.py:75
Sparse Core Ops, SparseCore 0:
  10.8 64.5 all-gather.4
  100.7 148.0 reduce-scatter.6
  331.7 164.4 all-gather.2
  511.1 97.0 reduce-scatter.4
where the time goes:
time: 615 us
  waiting for transfers between devices  530 us (86%)
  matrix products  28.9 us (5%)
  starting transfers between devices  19.9 us (3%)
  local copies, waits for them, and re-layouts  18.2 us (3%)
  between operations  13.8 us (2%)
    all_gather x1, waiting for transfers between devices, on_device(): lax.all_gather(rotated, 'dp', axis=0, tiled=True)  165 us
    unnamed x5, waiting for transfers between devices  149 us
    reduce_scatter x1, waiting for transfers between devices, on_device(): lax.psum_scatter(partial_value.astype(jnp.bfloat16), 'tensor', scatter_di...  95.3 us
    all_gather x1, waiting for transfers between devices, on_device(): grad_rows = lax.all_gather(grad_out, 'tensor', axis=0, tiled=True)  66.6 us
    ppermute x8, waiting for transfers between devices, from_partner(): lax.ppermute(value, axis, [(i, i ^ 1 << stride) for i in range(lax.axis_s...  54.5 us
    ppermute x8, starting transfers between devices, from_partner(): lax.ppermute(value, axis, [(i, i ^ 1 << stride) for i in range(lax.axis_s...  19.7 us
    unnamed x15, local copies, waits for them, and re-layouts  17.7 us
    dot_general x1, matrix products, on_device(): jnp.dot(lax.all_gather(rotated, 'dp', axis=0, tiled=True), weight, prefer...  14.7 us
  transfers between devices with their start and end apart: 12, of which 12 were waited for; matrix products, arithmetic and copies ran while one was open for 1% of the time, Pallas kernels for 0%

commit v1 on v0

v1 whole, which is shorter than its diff:
```python
import math

import jax
import jax.numpy as jnp
import numpy as np
from jax import lax
from jax.experimental import pallas as pl
from jax.experimental.pallas import tpu as pltpu
from jax.sharding import PartitionSpec as P

MESH = pl.DeviceIdType.MESH
F32, BF16 = jnp.float32, jnp.bfloat16
B = 128
FL, DL = 1664, 1024
NZ, NT = 8, 16
HALF = 896
WIDTHS = (896, 768)
ROWS = NZ * B
CHUNKS = tuple((k * 256, min(256, FL - k * 256)) for k in range(7))


def dot(a, b):
    return jnp.dot(a, b, preferred_element_type=F32)


def dot_t(a, b):
    return lax.dot_general(a, b, (((1,), (1,)), ((), ())), preferred_element_type=F32)


def block_rows(index, size=B):
    return pl.ds(pl.multiple_of(index * size, size), size)


def kernel(
    gate_ref, up_ref, codes_ref, scales_ref, grad_ref, had_ref,
    out_ref, gate_grad_ref, up_grad_ref,
    codes_v, w_all, hid, mix_in, mix_out, acts, grads,
    cpart, crecv, csum, yrecv, xsend, xrecv, osend, oacc,
    back, ring, rot_grad, grad_hid,
    code_sem, w_s, w_r, a_s, a_r, ag_s, ag_r,
    gd_s, gd_r, gx_s, gx_r, gy_s, gy_r, gc_s, gc_r,
    c_s, c_r, y_s, y_r, x_s, x_r, o_s, o_r, rs_s, rs_r,
):
    d, t = lax.axis_index("dp"), lax.axis_index("tensor")
    z, xl = lax.div(d, 2), lax.rem(d, 2)
    y, xh, core = lax.div(t, 4), lax.rem(lax.div(t, 2), 2), lax.rem(t, 2)

    def dev(z_=z, xl_=xl, y_=y, xh_=xh, c_=core):
        return (z_ * 2 + xl_, y_ * 4 + xh_ * 2 + c_)

    def zmod(v):
        return lax.rem(v + NZ, NZ)

    partner = dev(xl_=1 - xl)
    diagonal = dev(xl_=1 - xl, c_=1 - core)
    sibling = dev(c_=1 - core)
    across = dev(xh_=1 - xh)
    z_next = (dev(z_=zmod(z + 1)), dev(z_=zmod(z - 1)))
    y_peer = [dev(y_=lax.rem(y + r, 4)) for r in range(4)]
    sent = []

    def copy(src, dst, send, recv, device):
        return pltpu.make_async_remote_copy(
            src_ref=src, dst_ref=dst, send_sem=send, recv_sem=recv, device_id=device, device_id_type=MESH
        )

    def push(*args):
        op = copy(*args)
        op.start()
        sent.append(op)

    def arrived(dst, send, recv):
        copy(dst, dst, send, recv, sibling).wait_recv()

    fetch = pltpu.make_async_copy(codes_ref, codes_v, code_sem)
    fetch.start()

    barrier = pltpu.get_barrier_semaphore()

    def greet(j, carry):
        pl.semaphore_signal(barrier, inc=1, device_id=(d, lax.rem(t + j, NT)), device_id_type=MESH)
        return carry

    lax.fori_loop(1, NT, greet, 0)
    for device in (*z_next, partner, diagonal):
        pl.semaphore_signal(barrier, inc=1, device_id=device, device_id_type=MESH)

    def hidden_rows(i, carry):
        rows = block_rows(i, 16)
        gate = gate_ref[rows, :].astype(F32)
        value = (gate * jax.nn.sigmoid(gate) * up_ref[rows, :].astype(F32)).astype(BF16)
        hid[0, rows, :] = value[:, :HALF]
        hid[1, rows, : WIDTHS[1]] = value[:, HALF:]
        hid[1, rows, WIDTHS[1] :] = jnp.zeros((16, HALF - WIDTHS[1]), BF16)
        rot_grad[1, rows, WIDTHS[1] :] = jnp.zeros((16, HALF - WIDTHS[1]), BF16)
        return carry

    lax.fori_loop(0, 8, hidden_rows, 0)
    pl.semaphore_wait(barrier, NT - 1 + 4)

    def out_copy(i, src, j):
        p = lax.rem(t + j, NT)
        piece = src.at[lax.rem(p, 2), block_rows(lax.div(p, 2), 16), :]
        return copy(piece, mix_in.at[i, t], a_s.at[2 * i, j], a_r.at[2 * i, j], (d, p))

    def scatter(i, src):
        def step(j, carry):
            out_copy(i, src, j).start()
            return carry

        lax.fori_loop(1, NT, step, 0)
        mix_in[i, t] = src[core, block_rows(lax.div(t, 2), 16), :]

    def scattered(i):
        def step(j, carry):
            p = lax.rem(t - j + NT, NT)
            arrived(mix_in.at[i, p], a_s.at[2 * i, j], a_r.at[2 * i, j])
            return carry

        lax.fori_loop(1, NT, step, 0)

    def mix(i):
        had = had_ref[...]
        for b in range(HALF // B):
            cols = slice(b * B, (b + 1) * B)
            mixed = dot(mix_in[i, :, :, cols].reshape(256, B), had)
            parts = [mixed[g * 16 : (g + 1) * 16] for g in range(NT)]
            for bit in (1, 2, 4, 8):
                parts = [parts[g] + parts[g ^ bit] if not g & bit else parts[g ^ bit] - parts[g] for g in range(NT)]
            for g in range(NT):
                mix_out[i, g, :, cols] = (parts[g] * (1.0 / math.sqrt(NT * B))).astype(BF16)

    def back_copy(i, dst, base, j):
        p = lax.rem(t + j, NT)
        landing = dst.at[core, block_rows(base + lax.div(t, 2), 16), :]
        return copy(mix_out.at[i, p], landing, a_s.at[2 * i + 1, j], a_r.at[2 * i + 1, j], (d, p))

    def gather(i, dst, base):
        def step(j, carry):
            back_copy(i, dst, base, j).start()
            return carry

        lax.fori_loop(1, NT, step, 0)
        dst[core, block_rows(base + lax.div(t, 2), 16), :] = mix_out[i, t]

    def gathered(i, dst, base):
        def step(j, carry):
            p = lax.rem(t - j + NT, NT)
            landing = dst.at[lax.rem(p, 2), block_rows(base + lax.div(p, 2), 16), :]
            arrived(landing, a_s.at[2 * i + 1, j], a_r.at[2 * i + 1, j])
            return carry

        lax.fori_loop(1, NT, step, 0)

    scatter(0, hid)

    own_rows, across_rows = block_rows(2 * y + xh), block_rows(2 * y + 1 - xh)
    diagonal_copy = copy(grad_ref, grads.at[xl, own_rows, :], gd_s, gd_r, diagonal)

    @pl.when(core != xl)
    def _():
        diagonal_copy.start()

    @pl.when(core == xl)
    def _():
        grads[core, own_rows, :] = grad_ref[...]

    fetch.wait()

    def weight_copy(k):
        start, size = CHUNKS[k]
        piece = w_all.at[xl, pl.ds(start, size), :]
        return (piece, piece, w_s.at[k], w_r.at[k], partner)

    def weight_arrived(k):
        start, size = CHUNKS[k]
        arrived(w_all.at[1 - xl, pl.ds(start, size), :], w_s.at[k], w_r.at[k])

    def dequantize(k):
        start, size = CHUNKS[k]

        def one(i, carry):
            rows = block_rows(i)
            for j in range(DL // B):
                cols = slice(j * B, (j + 1) * B)
                w_all[xl, rows, cols] = (codes_v[rows, cols].astype(F32) * scales_ref[i, j]).astype(BF16)
            return carry

        lax.fori_loop(start // B, (start + size) // B, one, 0)

    for k in range(len(CHUNKS)):
        dequantize(k)
        push(*weight_copy(k))

    def grad_own():
        @pl.when(core != xl)
        def _():
            arrived(grads.at[core, own_rows, :], gd_s, gd_r)

        mine = grads.at[core, own_rows, :]
        push(mine, mine, gx_s, gx_r, across)
        for r in (1, 3, 2):
            push(mine, mine, gy_s.at[0, r], gy_r.at[0, r], y_peer[r])
        push(mine, mine, gc_s.at[0, 0], gc_r.at[0, 0], sibling)

    def grad_across():
        piece = grads.at[core, across_rows, :]
        arrived(piece, gx_s, gx_r)
        for r in (1, 3, 2):
            push(piece, piece, gy_s.at[1, r], gy_r.at[1, r], y_peer[r])
        push(piece, piece, gc_s.at[1, 0], gc_r.at[1, 0], sibling)

    def grad_y(f, r):
        source = lax.rem(y - r + 4, 4)
        piece = grads.at[core, block_rows(2 * source + (1 - xh if f else xh)), :]
        arrived(piece, gy_s.at[f, r], gy_r.at[f, r])
        push(piece, piece, gc_s.at[f, r], gc_r.at[f, r], sibling)

    def grad_done():
        for f in range(2):
            for r in range(4):
                source = lax.rem(y - r + 4, 4)
                piece = grads.at[1 - core, block_rows(2 * source + (1 - xh if f else xh)), :]
                arrived(piece, gc_s.at[f, r], gc_r.at[f, r])

    def ag_copy(way, s, group):
        block = zmod(z - s) if way == 0 else zmod(z + s)
        piece = acts.at[group, block_rows(block), pl.ds(0, WIDTHS[group])]
        return (piece, piece, ag_s.at[way, s, group], ag_r.at[way, s, group], z_next[way])

    def ag_step(s):
        for way in range(2):
            for group in range(2):
                if s and (s < 4 or way == group):
                    block = zmod(z - s) if way == 0 else zmod(z + s)
                    piece = acts.at[group, block_rows(block), pl.ds(0, WIDTHS[group])]
                    arrived(piece, ag_s.at[way, s - 1, group], ag_r.at[way, s - 1, group])
                if s < 3 or (s == 3 and way == group):
                    push(*ag_copy(way, s, group))

    def rs_push(way, k, s):
        size = CHUNKS[k][1]
        block = zmod(z + 4 - s) if way == 0 else zmod(z - 4 + s)
        if s == 0:
            piece = back.at[k, block_rows(2 * block + way, 64), pl.ds(0, size)]
            landing = ring.at[way, k, 0, pl.ds(0, 64), pl.ds(0, size)]
        else:
            piece = back.at[k, block_rows(block), pl.ds(0, size)]
            landing = ring.at[way, k, s, :, pl.ds(0, size)]
        push(piece, landing, rs_s.at[way, k, s], rs_r.at[way, k, s], z_next[way])

    def rs_arrived(way, k, s):
        size = CHUNKS[k][1]
        landing = ring.at[way, k, s, pl.ds(0, B if s else 64), pl.ds(0, size)]
        arrived(landing, rs_s.at[way, k, s], rs_r.at[way, k, s])

    def back_step(k, s):
        start, size = CHUNKS[k]
        cols = slice(0, size)
        if s == 0:
            weight_arrived(k)

            def product(m, carry):
                rows = block_rows(m, 256)
                term = dot_t(grads[0, rows, :], w_all[0, start : start + size, :])
                term = term + dot_t(grads[1, rows, :], w_all[1, start : start + size, :])
                back[k, rows, cols] = term.astype(BF16)
                return carry

            lax.fori_loop(0, ROWS // 256, product, 0)
            for way in range(2):
                rs_push(way, k, 0)
        elif s < 4:
            for way in range(2):
                rs_arrived(way, k, s - 1)
                block = zmod(z + 4 - s) if way == 0 else zmod(z - 4 + s)
                if s == 1:
                    rows = block_rows(2 * block + way, 64)
                    came = ring[way, k, 0, :64, cols]
                else:
                    rows = block_rows(block)
                    came = ring[way, k, s - 1, :, cols]
                back[k, rows, cols] = (back[k, rows, cols].astype(F32) + came.astype(F32)).astype(BF16)
                rs_push(way, k, s)
        else:
            for way in range(2):
                rs_arrived(way, k, 3)
            total = back[k, block_rows(z), cols].astype(F32)
            total = total + ring[0, k, 3, :, cols].astype(F32) + ring[1, k, 3, :, cols].astype(F32)
            total = total.astype(BF16)
            for b in range(size // B):
                group, place = divmod(start // B + b, HALF // B)
                rot_grad[group, :, place * B : (place + 1) * B] = total[:, b * B : (b + 1) * B]

    def out_product(turn):
        width = xl if turn == 0 else 1 - xl

        def one(n, carry):
            r = lax.rem(n + 1, 4)
            rows = block_rows(lax.rem(y + r, 4), 256)
            for h in range(2):
                cols = slice(h * 512, (h + 1) * 512)
                term = dot(acts[0, rows, :], w_all[width, :HALF, cols])
                term = term + dot(acts[1, rows, : WIDTHS[1]], w_all[width, HALF:, cols])
                cpart[turn, h, rows, :] = term.astype(BF16)
            copy(cpart.at[turn, 1 - core, rows, :], crecv.at[turn, rows, :], c_s.at[turn, r], c_r.at[turn, r], sibling).start()
            return carry

        lax.fori_loop(0, 4, one, 0)
        for r in range(4):
            rows = block_rows(lax.rem(y + r, 4), 256)
            sent.append(copy(cpart.at[turn, 1 - core, rows, :], crecv.at[turn, rows, :], c_s.at[turn, r], c_r.at[turn, r], sibling))

    def out_core_sum(turn):
        for r in (1, 2, 3, 0):
            rows = block_rows(lax.rem(y + r, 4), 256)
            arrived(crecv.at[turn, rows, :], c_s.at[turn, r], c_r.at[turn, r])
            csum[turn, rows, :] = (cpart[turn, core, rows, :].astype(F32) + crecv[turn, rows, :].astype(F32)).astype(BF16)
            if r:
                push(csum.at[turn, rows, :], yrecv.at[turn, r - 1], y_s.at[turn, r], y_r.at[turn, r], y_peer[r])

    def out_y_part(turn, side):
        total = csum[turn, block_rows(2 * y + side), :].astype(F32)
        for r in range(3):
            total = total + yrecv[turn, r, block_rows(side), :].astype(F32)
        return total

    def out_y_sum(turn):
        for r in range(1, 4):
            arrived(yrecv.at[turn, r - 1], y_s.at[turn, r], y_r.at[turn, r])
        xsend[turn] = out_y_part(turn, 1 - xh).astype(BF16)
        push(xsend.at[turn], xrecv.at[turn], x_s.at[turn], x_r.at[turn], across)

    out_copies = [
        copy(osend.at[0], oacc.at[core], o_s.at[0], o_r.at[core], sibling),
        copy(osend.at[1], oacc.at[core], o_s.at[1], o_r.at[core], dev(xl_=1 - xl, c_=xl)),
    ]

    def out_place(turn):
        arrived(xrecv.at[turn], x_s.at[turn], x_r.at[turn])
        osend[turn] = (out_y_part(turn, xh) + xrecv[turn].astype(F32)).astype(BF16)
        if turn == 0:

            @pl.when(core == xl)
            def _():
                oacc[core] = osend[0]

            @pl.when(core != xl)
            def _():
                out_copies[0].start()
        else:
            out_copies[1].start()

    def out_done():
        @pl.when(core == xl)
        def _():
            arrived(oacc.at[1 - core], o_s.at[0], o_r.at[1 - core])

        @pl.when(core != xl)
        def _():
            for h in range(2):
                arrived(oacc.at[h], o_s.at[0], o_r.at[h])

        for h in range(2):
            out_ref[:, h * 512 : (h + 1) * 512] = oacc[h]

    grad_own()
    scattered(0)
    mix(0)
    gather(0, acts, z * 8)
    grad_across()
    gathered(0, acts, z * 8)
    ag_step(0)
    for r in (1, 3, 2):
        grad_y(0, r)
    ag_step(1)
    for r in (1, 3, 2):
        grad_y(1, r)
    grad_done()
    ag_step(2)
    back_step(0, 0)
    ag_step(3)
    back_step(0, 1)
    back_step(1, 0)
    ag_step(4)
    early = [lambda: out_product(0), lambda: out_core_sum(0), lambda: out_y_sum(0), lambda: out_place(0)]
    n = len(CHUNKS)
    for tick in range(2, n + 4):
        for s in (4, 3, 2, 1, 0):
            k = tick - s
            if 0 <= k < n and (k, s) != (0, 1):
                back_step(k, s)
        if tick == n - 1:
            out_product(1)
        elif tick == n:
            out_core_sum(1)
        elif tick == n + 2:
            out_y_sum(1)
        if early:
            early.pop(0)()
    scatter(1, rot_grad)
    out_place(1)
    scattered(1)
    mix(1)
    gather(1, grad_hid, 0)
    out_done()
    gathered(1, grad_hid, 0)

    def grad_rows(i, carry):
        rows = block_rows(i, 16)
        gate, up = gate_ref[rows, :].astype(F32), up_ref[rows, :].astype(F32)
        sig = jax.nn.sigmoid(gate)
        silu, slope = gate * sig, up * sig * (1.0 + gate * (1.0 - sig))
        for group in range(2):
            cols = slice(group * HALF, group * HALF + WIDTHS[group])
            value = grad_hid[group, rows, : WIDTHS[group]].astype(F32)
            up_grad_ref[rows, cols] = (value * silu[:, cols]).astype(BF16)
            gate_grad_ref[rows, cols] = (value * slope[:, cols]).astype(BF16)
        return carry

    lax.fori_loop(0, 8, grad_rows, 0)

    for op in sent:
        op.wait_send()

    @pl.when(core != xl)
    def _():
        diagonal_copy.wait_send()
        out_copies[0].wait_send()

    out_copies[1].wait_send()

    def drain(j, carry):
        out_copy(0, hid, j).wait_send()
        out_copy(1, rot_grad, j).wait_send()
        back_copy(0, acts, z * 8, j).wait_send()
        back_copy(1, grad_hid, 0, j).wait_send()
        return carry

    lax.fori_loop(1, NT, drain, 0)


def hadamard():
    index = np.arange(B)
    bits = index[:, None] & index[None, :]
    parity = sum(bits >> s & 1 for s in range(7)) % 2
    return (1 - 2 * parity).astype(np.float32)


def on_device(gate_act, up_act, down_codes, down_scales, grad_out):
    vmem, dma = pltpu.VMEM, pltpu.SemaphoreType.DMA
    whole = pl.BlockSpec(memory_space=pltpu.VMEM)
    return pl.pallas_call(
        kernel,
        out_shape=(
            jax.ShapeDtypeStruct((B, DL), BF16),
            jax.ShapeDtypeStruct((B, FL), BF16),
            jax.ShapeDtypeStruct((B, FL), BF16),
        ),
        in_specs=[
            whole,
            whole,
            pl.BlockSpec(memory_space=pl.ANY),
            pl.BlockSpec(memory_space=pltpu.SMEM),
            whole,
            whole,
        ],
        out_specs=(whole, whole, whole),
        scratch_shapes=[
            vmem((FL, DL), BF16),
            vmem((2, FL, DL), BF16),
            vmem((2, B, HALF), BF16),
            vmem((2, NT, 16, HALF), BF16),
            vmem((2, NT, 16, HALF), BF16),
            vmem((2, ROWS, HALF), BF16),
            vmem((2, ROWS, DL), BF16),
            vmem((2, 2, ROWS, 512), BF16),
            vmem((2, ROWS, 512), BF16),
            vmem((2, ROWS, 512), BF16),
            vmem((2, 3, 256, 512), BF16),
            vmem((2, B, 512), BF16),
            vmem((2, B, 512), BF16),
            vmem((2, B, 512), BF16),
            vmem((2, B, 512), BF16),
            vmem((7, ROWS, 256), BF16),
            vmem((2, 7, 4, B, 256), BF16),
            vmem((2, B, HALF), BF16),
            vmem((2, B, HALF), BF16),
            dma,
            dma((7,)), dma((7,)),
            dma((4, NT)), dma((4, NT)),
            dma((2, 4, 2)), dma((2, 4, 2)),
            dma, dma,
            dma, dma,
            dma((2, 4)), dma((2, 4)),
            dma((2, 4)), dma((2, 4)),
            dma((2, 4)), dma((2, 4)),
            dma((2, 4)), dma((2, 4)),
            dma((2,)), dma((2,)),
            dma((2,)), dma((2,)),
            dma((2, 7, 4)), dma((2, 7, 4)),
        ],
        compiler_params=pltpu.CompilerParams(
            collective_id=0, has_side_effects=True, vmem_limit_bytes=56 * 1024 * 1024
        ),
    )(gate_act, up_act, down_codes, down_scales, grad_out, jnp.asarray(hadamard(), BF16))


def solution(mesh):
    return jax.shard_map(
        on_device,
        mesh=mesh,
        in_specs=(
            P("dp", "tensor"),
            P("dp", "tensor"),
            P("tensor", "dp"),
            P("tensor", "dp"),
            P("tensor", "dp"),
        ),
        out_specs=(P("tensor", "dp"), P("dp", "tensor"), P("dp", "tensor")),
        check_vma=False,
    )
```

time: 615 us -> 225 us (0.37)
  waiting for transfers between devices: 530 us -> 0 us
  Pallas kernels: 0 us -> 218 us
  matrix products: 28.9 us -> 0 us
  starting transfers between devices: 19.9 us -> 0 us
  between operations: 13.8 us -> 0.64 us
  local copies, waits for them, and re-layouts: 18.2 us -> 6.62 us
    all_gather x2 -> x0, waiting for transfers between devices: 231 us -> none  [the longest x1 165 us: on_device(): lax.all_gather(rotated, 'dp', axis=0, tiled=True)]
    pallas_call x0 -> x1, Pallas kernels: none -> 218 us  [on_device(): pl.pallas_call(kernel, out_shape=(jax.ShapeDtypeStruct((B, DL), BF16), ja...]
    unnamed x5 -> x0, waiting for transfers between devices: 149 us -> none
    reduce_scatter x1 -> x0, waiting for transfers between devices: 95.3 us -> none  [on_device(): lax.psum_scatter(partial_value.astype(jnp.bfloat16), 'tensor', scatter_di...]
    ppermute x8 -> x0, waiting for transfers between devices: 54.5 us -> none  [from_partner(): lax.ppermute(value, axis, [(i, i ^ 1 << stride) for i in range(lax.axis_s...]
    dot_general x4 -> x0, matrix products: 28.9 us -> none  [the longest x1 14.7 us: on_device(): jnp.dot(lax.all_gather(rotated, 'dp', axis=0, tiled=True), weight, prefer...]
    ppermute x8 -> x0, starting transfers between devices: 19.7 us -> none  [from_partner(): lax.ppermute(value, axis, [(i, i ^ 1 << stride) for i in range(lax.axis_s...]
    unnamed x15 -> x4, local copies, waits for them, and re-layouts: 17.7 us -> 6.62 us
  transfers between devices with their start and end apart: 12 -> 0, of which waited for: 12 -> 0; matrix products, arithmetic and copies ran while one was open for 1% -> 0% of each run, Pallas kernels for 0% -> 0%
where the time goes in v1:
time: 225 us
  Pallas kernels  218 us (97%)
  local copies, waits for them, and re-layouts  6.62 us (3%)
    pallas_call x1, Pallas kernels, on_device(): pl.pallas_call(kernel, out_shape=(jax.ShapeDtypeStruct((B, DL), BF16), ja...  218 us
    unnamed x4, local copies, waits for them, and re-layouts  6.62 us

profile of v1, /device:TPU:1, one launch (start us, length us, event | category | flops | bytes accessed | tf_op | source)
XLA Modules:
  0.0 225.2 jit_solution(12308897307933754113)
XLA Ops:
  0.6 1.4 copy.9.scales_ref
  2.0 217.9 %shard_map.85 = (bf16[128,1024]{1,0:T(8,128)(2,1)}, bf16[128,1664]{1,0:T(8,128)(2,1)}, bf16[128,1664]{1,0:T(8,128)(2,1)}) custom-call(bf16[128,1664]{1,0:T(8,128)(2,1)} %gate_ref.1, bf16[128,1664]{1,0:T(8,128)(2,1)} %up_ref.1, bf16[1664,1024]{1,0:T(8,128)(2,1)} %codes_ref.1, f32[13,8]{1,0:T(8,128)} %copy.9.scales_ref, bf16[128,1024]{1,0:T(8,128)(2,1)} %grad_ref.1, ...), custom_call_target="tpu_custom_call" | custom-call | tf_op jit(solution)/shard_map/pallas_call | solution.py:453
  219.9 1.7 copy.13
  221.6 1.8 copy.14
  223.4 1.8 copy.15

commit v2 on v1

--- a/solution.py
+++ b/solution.py
@@ -16,7 +16,7 @@
 HALF = 896
 WIDTHS = (896, 768)
 ROWS = NZ * B
-CHUNKS = tuple((k * 256, min(256, FL - k * 256)) for k in range(7))
+CHUNKS = ((0, B),) + tuple((B + k * 256, 256) for k in range(6))
 
 
 def dot(a, b):
@@ -33,7 +33,7 @@
 
 def kernel(
     gate_ref, up_ref, codes_ref, scales_ref, grad_ref, had_ref,
-    out_ref, gate_grad_ref, up_grad_ref,
+    out_ref, grad_ref_out,
     codes_v, w_all, hid, mix_in, mix_out, acts, grads,
     cpart, crecv, csum, yrecv, xsend, xrecv, osend, oacc,
     back, ring, rot_grad, grad_hid,
@@ -111,6 +111,22 @@
         lax.fori_loop(1, NT, step, 0)
         mix_in[i, t] = src[core, block_rows(lax.div(t, 2), 16), :]
 
+    def to_group(group, body):
+        other = lax.rem(core + group, 2)
+
+        def step(i, carry):
+            body(2 * i + other)
+            return carry
+
+        lax.fori_loop(1 - other, NT // 2, step, 0)
+
+    def scatter_group(src, group):
+        to_group(group, lambda j: out_copy(1, src, j).start())
+
+        @pl.when(core == group)
+        def _():
+            mix_in[1, t] = src[core, block_rows(lax.div(t, 2), 16), :]
+
     def scattered(i):
         def step(j, carry):
             p = lax.rem(t - j + NT, NT)
@@ -152,20 +168,9 @@
 
         lax.fori_loop(1, NT, step, 0)
 
-    scatter(0, hid)
-
     own_rows, across_rows = block_rows(2 * y + xh), block_rows(2 * y + 1 - xh)
     diagonal_copy = copy(grad_ref, grads.at[xl, own_rows, :], gd_s, gd_r, diagonal)
 
-    @pl.when(core != xl)
-    def _():
-        diagonal_copy.start()
-
-    @pl.when(core == xl)
-    def _():
-        grads[core, own_rows, :] = grad_ref[...]
-
-    fetch.wait()
 
     def weight_copy(k):
         start, size = CHUNKS[k]
@@ -179,18 +184,12 @@
     def dequantize(k):
         start, size = CHUNKS[k]
 
-        def one(i, carry):
-            rows = block_rows(i)
+        for i in range(start // B, (start + size) // B):
+            rows = slice(i * B, (i + 1) * B)
             for j in range(DL // B):
                 cols = slice(j * B, (j + 1) * B)
-                w_all[xl, rows, cols] = (codes_v[rows, cols].astype(F32) * scales_ref[i, j]).astype(BF16)
-            return carry
-
-        lax.fori_loop(start // B, (start + size) // B, one, 0)
-
-    for k in range(len(CHUNKS)):
-        dequantize(k)
-        push(*weight_copy(k))
+                scale = jnp.broadcast_to(scales_ref[j : j + 1, i : i + 1], (B, B))
+                w_all[xl, rows, cols] = (codes_v[rows, cols].astype(F32) * scale).astype(BF16)
 
     def grad_own():
         @pl.when(core != xl)
@@ -292,32 +291,26 @@
                 group, place = divmod(start // B + b, HALF // B)
                 rot_grad[group, :, place * B : (place + 1) * B] = total[:, b * B : (b + 1) * B]
 
-    def out_product(turn):
+    def out_core_copy(turn, r):
+        rows = block_rows(lax.rem(y + r, 4), 256)
+        return (cpart.at[turn, 1 - core, rows, :], crecv.at[turn, rows, :], c_s.at[turn, r], c_r.at[turn, r], sibling)
+
+    def out_product(turn, r):
         width = xl if turn == 0 else 1 - xl
-
-        def one(n, carry):
-            r = lax.rem(n + 1, 4)
-            rows = block_rows(lax.rem(y + r, 4), 256)
-            for h in range(2):
-                cols = slice(h * 512, (h + 1) * 512)
-                term = dot(acts[0, rows, :], w_all[width, :HALF, cols])
-                term = term + dot(acts[1, rows, : WIDTHS[1]], w_all[width, HALF:, cols])
-                cpart[turn, h, rows, :] = term.astype(BF16)
-            copy(cpart.at[turn, 1 - core, rows, :], crecv.at[turn, rows, :], c_s.at[turn, r], c_r.at[turn, r], sibling).start()
-            return carry
-
-        lax.fori_loop(0, 4, one, 0)
-        for r in range(4):
-            rows = block_rows(lax.rem(y + r, 4), 256)
-            sent.append(copy(cpart.at[turn, 1 - core, rows, :], crecv.at[turn, rows, :], c_s.at[turn, r], c_r.at[turn, r], sibling))
-
-    def out_core_sum(turn):
-        for r in (1, 2, 3, 0):
-            rows = block_rows(lax.rem(y + r, 4), 256)
-            arrived(crecv.at[turn, rows, :], c_s.at[turn, r], c_r.at[turn, r])
-            csum[turn, rows, :] = (cpart[turn, core, rows, :].astype(F32) + crecv[turn, rows, :].astype(F32)).astype(BF16)
-            if r:
-                push(csum.at[turn, rows, :], yrecv.at[turn, r - 1], y_s.at[turn, r], y_r.at[turn, r], y_peer[r])
+        rows = block_rows(lax.rem(y + r, 4), 256)
+        for h in range(2):
+            cols = slice(h * 512, (h + 1) * 512)
+            term = dot(acts[0, rows, :], w_all[width, :HALF, cols])
+            term = term + dot(acts[1, rows, : WIDTHS[1]], w_all[width, HALF:, cols])
+            cpart[turn, h, rows, :] = term.astype(BF16)
+        push(*out_core_copy(turn, r))
+
+    def out_core_sum(turn, r):
+        rows = block_rows(lax.rem(y + r, 4), 256)
+        arrived(crecv.at[turn, rows, :], c_s.at[turn, r], c_r.at[turn, r])
+        csum[turn, rows, :] = (cpart[turn, core, rows, :].astype(F32) + crecv[turn, rows, :].astype(F32)).astype(BF16)
+        if r:
+            push(csum.at[turn, rows, :], yrecv.at[turn, r - 1], y_s.at[turn, r], y_r.at[turn, r], y_peer[r])
 
     def out_y_part(turn, side):
         total = csum[turn, block_rows(2 * y + side), :].astype(F32)
@@ -361,13 +354,27 @@
             for h in range(2):
                 arrived(oacc.at[h], o_s.at[0], o_r.at[h])
 
-        for h in range(2):
-            out_ref[:, h * 512 : (h + 1) * 512] = oacc[h]
-
+    scatter(0, hid)
+
+    @pl.when(core != xl)
+    def _():
+        diagonal_copy.start()
+
+    @pl.when(core == xl)
+    def _():
+        grads[core, own_rows, :] = grad_ref[...]
+
+    fetch.wait()
+    dequantize(0)
+    push(*weight_copy(0))
+    for k in range(1, 7):
+        dequantize(k)
     grad_own()
     scattered(0)
     mix(0)
     gather(0, acts, z * 8)
+    for k in range(1, 7):
+        push(*weight_copy(k))
     grad_across()
     gathered(0, acts, z * 8)
     ag_step(0)
@@ -383,42 +390,64 @@
     back_step(0, 1)
     back_step(1, 0)
     ag_step(4)
-    early = [lambda: out_product(0), lambda: out_core_sum(0), lambda: out_y_sum(0), lambda: out_place(0)]
     n = len(CHUNKS)
-    for tick in range(2, n + 4):
+
+    def tick(i):
         for s in (4, 3, 2, 1, 0):
-            k = tick - s
-            if 0 <= k < n and (k, s) != (0, 1):
-                back_step(k, s)
-        if tick == n - 1:
-            out_product(1)
-        elif tick == n:
-            out_core_sum(1)
-        elif tick == n + 2:
-            out_y_sum(1)
-        if early:
-            early.pop(0)()
-    scatter(1, rot_grad)
+            if 0 <= i - s < n and (i - s, s) != (0, 1):
+                back_step(i - s, s)
+
+    tick(2)
+    for r in (1, 2):
+        out_product(0, r)
+    tick(3)
+    for r in (3, 0):
+        out_product(0, r)
+    for r in (1, 2):
+        out_core_sum(0, r)
+    tick(4)
+    for r in (3, 0):
+        out_core_sum(0, r)
+    tick(5)
+    out_y_sum(0)
+    tick(6)
+    out_product(1, 1)
+    tick(7)
+    scatter_group(rot_grad, 0)
+    out_core_sum(1, 1)
+    out_product(1, 2)
+    tick(8)
+    out_core_sum(1, 2)
+    out_product(1, 3)
+    tick(9)
+    out_core_sum(1, 3)
+    out_product(1, 0)
+
+    @pl.when(core == 0)
+    def _():
+        scattered(1)
+        mix(1)
+        gather(1, grad_hid, 0)
+
+    tick(10)
+    scatter_group(rot_grad, 1)
+    out_core_sum(1, 0)
+    out_y_sum(1)
+    out_place(0)
+
+    @pl.when(core == 1)
+    def _():
+        scattered(1)
+        mix(1)
+        gather(1, grad_hid, 0)
+
     out_place(1)
-    scattered(1)
-    mix(1)
-    gather(1, grad_hid, 0)
     out_done()
     gathered(1, grad_hid, 0)
-
-    def grad_rows(i, carry):
-        rows = block_rows(i, 16)
-        gate, up = gate_ref[rows, :].astype(F32), up_ref[rows, :].astype(F32)
-        sig = jax.nn.sigmoid(gate)
-        silu, slope = gate * sig, up * sig * (1.0 + gate * (1.0 - sig))
-        for group in range(2):
-            cols = slice(group * HALF, group * HALF + WIDTHS[group])
-            value = grad_hid[group, rows, : WIDTHS[group]].astype(F32)
-            up_grad_ref[rows, cols] = (value * silu[:, cols]).astype(BF16)
-            gate_grad_ref[rows, cols] = (value * slope[:, cols]).astype(BF16)
-        return carry
-
-    lax.fori_loop(0, 8, grad_rows, 0)
+    for h in range(2):
+        out_ref[:, h * 512 : (h + 1) * 512] = oacc[h]
+    grad_ref_out[:, :HALF] = grad_hid[0]
+    grad_ref_out[:, HALF:] = grad_hid[1, :, : WIDTHS[1]]
 
     for op in sent:
         op.wait_send()
@@ -450,22 +479,11 @@
 def on_device(gate_act, up_act, down_codes, down_scales, grad_out):
     vmem, dma = pltpu.VMEM, pltpu.SemaphoreType.DMA
     whole = pl.BlockSpec(memory_space=pltpu.VMEM)
-    return pl.pallas_call(
+    layer_output, grad_hidden = pl.pallas_call(
         kernel,
-        out_shape=(
-            jax.ShapeDtypeStruct((B, DL), BF16),
-            jax.ShapeDtypeStruct((B, FL), BF16),
-            jax.ShapeDtypeStruct((B, FL), BF16),
-        ),
-        in_specs=[
-            whole,
-            whole,
-            pl.BlockSpec(memory_space=pl.ANY),
-            pl.BlockSpec(memory_space=pltpu.SMEM),
-            whole,
-            whole,
-        ],
-        out_specs=(whole, whole, whole),
+        out_shape=(jax.ShapeDtypeStruct((B, DL), BF16), jax.ShapeDtypeStruct((B, FL), BF16)),
+        in_specs=[whole, whole, pl.BlockSpec(memory_space=pl.ANY), whole, whole, whole],
+        out_specs=(whole, whole),
         scratch_shapes=[
             vmem((FL, DL), BF16),
             vmem((2, FL, DL), BF16),
@@ -503,7 +521,13 @@
         compiler_params=pltpu.CompilerParams(
             collective_id=0, has_side_effects=True, vmem_limit_bytes=56 * 1024 * 1024
         ),
-    )(gate_act, up_act, down_codes, down_scales, grad_out, jnp.asarray(hadamard(), BF16))
+    )(gate_act, up_act, down_codes, down_scales.T, grad_out, jnp.asarray(hadamard(), BF16))
+    grad_hidden = grad_hidden.astype(F32)
+    gate, up = gate_act.astype(F32), up_act.astype(F32)
+    sig = jax.nn.sigmoid(gate)
+    up_grad = (grad_hidden * (gate * sig)).astype(BF16)
+    gate_grad = (grad_hidden * up * sig * (1.0 + gate * (1.0 - sig))).astype(BF16)
+    return (layer_output, gate_grad, up_grad)
 
 
 def solution(mesh):

time: 225 us -> 150 us (0.67)
  Pallas kernels: 218 us -> 145 us
  local copies, waits for them, and re-layouts: 6.62 us -> 1.68 us
  other arithmetic: 0 us -> 2.37 us
    pallas_call x1, Pallas kernels: 218 us -> 145 us  [on_device(): pl.pallas_call(kernel, out_shape=(jax.ShapeDtypeStruct((B, DL), BF16), ja...]
    unnamed x4 -> x5, local copies, waits for them, and re-layouts: 6.62 us -> 1.68 us
    convert_element_type x0 -> x1, other arithmetic: none -> 2.37 us  [on_device(): up_grad = (grad_hidden * (gate * sig)).astype(BF16)]
where the time goes in v2:
time: 150 us; the launch traced here: 149 us
  Pallas kernels  145 us (97%)
  other arithmetic  2.37 us (2%)
  local copies, waits for them, and re-layouts  1.68 us (1%)
    pallas_call x1, Pallas kernels, on_device(): pl.pallas_call(kernel, out_shape=(jax.ShapeDtypeStruct((B, DL), BF16), ja...  145 us

profile of v2, /device:TPU:1, one launch (start us, length us, event | category | flops | bytes accessed | tf_op | source)
XLA Modules:
  0.0 149.3 jit_solution(5606337336658587046)
XLA Ops:
  0.6 0.0 copy-start.1
  0.6 0.0 copy-start
  0.7 144.6 %shard_map.85 = (bf16[128,1024]{1,0:T(8,128)(2,1)}, bf16[128,1664]{1,0:T(8,128)(2,1)}) custom-call(bf16[128,1664]{1,0:T(8,128)(2,1)} %gate_ref.1, bf16[128,1664]{1,0:T(8,128)(2,1)} %up_ref.1, bf16[1664,1024]{1,0:T(8,128)(2,1)} %codes_ref.1, f32[8,13]{1,0:T(8,128)} %bitcast.1, bf16[128,1024]{1,0:T(8,128)(2,1)} %grad_ref.1, bf16[128,128]{1,0:T(8,128)(2,1)} %constant.4.clone.had_ref), custom_call_target="tpu_custom_call" | custom-call | tf_op jit(solution)/shard_map/pallas_call | solution.py:482
  145.3 0.0 copy-done.1
  145.3 0.0 copy-done
  145.3 2.4 %fusion.3 = (bf16[128,1664]{1,0:T(8,128)(2,1)}, bf16[128,1664]{1,0:T(8,128)(2,1)}) fusion(bf16[128,1664]{1,0:T(8,128)(2,1)} %get-tuple-element.6, bf16[128,1664]{1,0:T(8,128)(2,1)S(1)} %copy-done, bf16[128,1664]{1,0:T(8,128)(2,1)S(1)} %copy-done.1), kind=kLoop, calls=%fused_computation.8 | loop fusion | flops 3407872 | bytes 2129920 | tf_op jit(solution)/shard_map/convert_element_type | solution.py:528
  147.7 1.7 %copy.10 = bf16[128,1024]{1,0:T(8,128)(2,1)} copy(bf16[128,1024]{1,0:T(8,128)(2,1)} %get-tuple-element.12) | data formatting | bytes 524288
Async XLA Ops:
  0.6 144.6 %copy-start.1 = (bf16[128,1664]{1,0:T(8,128)(2,1)S(1)}, bf16[128,1664]{1,0:T(8,128)(2,1)}, u32[]{:S(2)}) copy-start(bf16[128,1664]{1,0:T(8,128)(2,1)} %up_ref.1) | copy-start | bytes 1277956
  0.6 144.6 %copy-start = (bf16[128,1664]{1,0:T(8,128)(2,1)S(1)}, bf16[128,1664]{1,0:T(8,128)(2,1)}, u32[]{:S(2)}) copy-start(bf16[128,1664]{1,0:T(8,128)(2,1)} %gate_ref.1) | copy-start | bytes 1277956

commit v3 on v2

v3 whole, which is shorter than its diff:
```python
import math

import jax
import jax.numpy as jnp
import numpy as np
from jax import lax
from jax.experimental import pallas as pl
from jax.experimental.pallas import tpu as pltpu
from jax.sharding import PartitionSpec as P

MESH = pl.DeviceIdType.MESH
F32, BF16 = jnp.float32, jnp.bfloat16
B = 128
FL, DL = 1664, 1024
NZ, NT = 8, 16
HALF = 896
WIDTHS = (896, 768)
ROWS = NZ * B
STRIPS = ((0, 256), (256, 256), (512, 256), (768, B), (896, 256), (1152, 256), (1408, B), (1536, B))
ORDER = tuple((k, h) for k in range(6) for h in range(2)) + tuple((k, h) for h in range(2) for k in range(6, 8))
CHUNKS = ((0, 512), (512, 384), (896, 256), (1152, 256), (1408, B), (1536, B))
STRIPS_OF = ((0, 1), (2, 3), (4,), (5,), (6,), (7,))
RING = 4
TURNS = ((0, 0, 512), (1, 0, 256), (1, 512, 256))
PIECES = ((0, 0, 896), (1, 0, 512), (1, 512, 256))


def dot(a, b):
    return jnp.dot(a, b, preferred_element_type=F32)


def dot_t(a, b):
    return lax.dot_general(a, b, (((1,), (1,)), ((), ())), preferred_element_type=F32)


def block_rows(index, size=B):
    return pl.ds(pl.multiple_of(index * size, size), size)


def kernel(
    gate_hbm, up_hbm, codes_hbm, scales_hbm, grad_hbm, had_hbm,
    out_ref, grad_ref_out,
    gate_ref, up_ref, codes_v, scales_ref, grad_ref, had_ref,
    w_all, hid, mix_in, mix_out, acts, grads,
    cpart, crecv, csum, yrecv, xsend, xrecv, osend, oacc,
    back0, back1, back2, back3, ring0, ring1, ring2, ring3, back_last, direct, rot_grad, grad_hid,
    in_sem, w_s, w_r, a_s, a_r, e_s, e_r, ag_s, ag_r,
    gd_s, gd_r, gx_s, gx_r, gy_s, gy_r, gc_s, gc_r,
    c_s, c_r, y_s, y_r, x_s, x_r, o_s, o_r, rs_s, rs_r, ds_s, ds_r,
):
    d, t = lax.axis_index("dp"), lax.axis_index("tensor")
    back, ring = (back0, back1, back2, back3), (ring0, ring1, ring2, ring3)
    z, xl = lax.div(d, 2), lax.rem(d, 2)
    y, xh, core = lax.div(t, 4), lax.rem(lax.div(t, 2), 2), lax.rem(t, 2)

    def dev(z_=z, xl_=xl, y_=y, xh_=xh, c_=core):
        return (z_ * 2 + xl_, y_ * 4 + xh_ * 2 + c_)

    def zmod(v):
        return lax.rem(v + NZ, NZ)

    partner = dev(xl_=1 - xl)
    diagonal = dev(xl_=1 - xl, c_=1 - core)
    sibling = dev(c_=1 - core)
    across = dev(xh_=1 - xh)
    z_next = (dev(z_=zmod(z + 1)), dev(z_=zmod(z - 1)))
    y_peer = [dev(y_=lax.rem(y + r, 4)) for r in range(4)]
    sent = []

    def copy(src, dst, send, recv, device):
        return pltpu.make_async_remote_copy(
            src_ref=src, dst_ref=dst, send_sem=send, recv_sem=recv, device_id=device, device_id_type=MESH
        )

    def push(*args):
        op = copy(*args)
        op.start()
        sent.append(op)

    def arrived(dst, send, recv):
        copy(dst, dst, send, recv, sibling).wait_recv()

    first = pl.ds(0, STRIPS[0][1])
    rest = pl.ds(STRIPS[0][1], FL - STRIPS[0][1])
    fetches = [
        pltpu.make_async_copy(src, dst, in_sem.at[i])
        for i, (src, dst) in enumerate((
            (scales_hbm, scales_ref),
            (codes_hbm.at[first, :], codes_v.at[first, :]),
            (gate_hbm, gate_ref),
            (up_hbm, up_ref),
            (grad_hbm, grad_ref),
            (codes_hbm.at[rest, :], codes_v.at[rest, :]),
            (had_hbm, had_ref),
        ))
    ]
    for fetch in fetches:
        fetch.start()

    barrier = pltpu.get_barrier_semaphore()

    def greet(j, carry):
        pl.semaphore_signal(barrier, inc=1, device_id=(d, lax.rem(t + j, NT)), device_id_type=MESH)
        return carry

    lax.fori_loop(1, NT, greet, 0)
    z_peer = [dev(z_=lax.rem(z + j, NZ)) for j in range(NZ)]
    for device in (*z_peer[1:], partner, diagonal):
        pl.semaphore_signal(barrier, inc=1, device_id=device, device_id_type=MESH)

    def weight_piece(width, k, h):
        start, size = STRIPS[k]
        return w_all.at[width, pl.ds(start, size), pl.ds(h * 512, 512)]

    def weight_push(k, h):
        push(weight_piece(xl, k, h), weight_piece(xl, k, h), w_s.at[h, k], w_r.at[h, k], partner)

    def weight_arrived(k, h):
        arrived(weight_piece(1 - xl, k, h), w_s.at[h, k], w_r.at[h, k])

    def dequantize(k):
        start, size = STRIPS[k]
        for i in range(start // B, (start + size) // B):
            rows = slice(i * B, (i + 1) * B)
            for j in range(DL // B):
                cols = slice(j * B, (j + 1) * B)
                scale = jnp.broadcast_to(scales_ref[j : j + 1, i : i + 1], (B, B))
                w_all[xl, rows, cols] = (codes_v[rows, cols].astype(F32) * scale).astype(BF16)

    fetches[0].wait()
    fetches[1].wait()
    dequantize(0)
    fetches[2].wait()
    fetches[3].wait()

    def hidden_rows(i, carry):
        rows = block_rows(i, 16)
        gate = gate_ref[rows, :].astype(F32)
        value = (gate * jax.nn.sigmoid(gate) * up_ref[rows, :].astype(F32)).astype(BF16)
        hid[0, rows, :] = value[:, :HALF]
        hid[1, rows, : WIDTHS[1]] = value[:, HALF:]
        hid[1, rows, WIDTHS[1] :] = jnp.zeros((16, HALF - WIDTHS[1]), BF16)
        rot_grad[1, rows, WIDTHS[1] :] = jnp.zeros((16, HALF - WIDTHS[1]), BF16)
        return carry

    lax.fori_loop(0, 8, hidden_rows, 0)
    pl.semaphore_wait(barrier, NT - 1 + NZ - 1 + 2)

    def sixteen(p):
        return block_rows(lax.div(p, 2), 16)

    def peers(body):
        def step(j, carry):
            body(j)
            return carry

        lax.fori_loop(1, NT, step, 0)

    def peers_of(group, body):
        other = lax.rem(core + group, 2)

        def step(i, carry):
            body(2 * i + other)
            return carry

        lax.fori_loop(1 - other, NT // 2, step, 0)

    def mix(i, start, size):
        had = had_ref[...]
        for b in range(start // B, (start + size) // B):
            cols = slice(b * B, (b + 1) * B)
            mixed = dot(mix_in[i, :, :, cols].reshape(256, B), had)
            parts = [mixed[g * 16 : (g + 1) * 16] for g in range(NT)]
            for bit in (1, 2, 4, 8):
                parts = [parts[g] + parts[g ^ bit] if not g & bit else parts[g ^ bit] - parts[g] for g in range(NT)]
            for g in range(NT):
                mix_out[i, g, :, cols] = (parts[g] * (1.0 / math.sqrt(NT * B))).astype(BF16)

    def first_copy(j):
        p = lax.rem(t + j, NT)
        return copy(hid.at[lax.rem(p, 2), sixteen(p), :], mix_in.at[0, t], a_s.at[0, j], a_r.at[0, j], (d, p))

    def first_back(j):
        p = lax.rem(t + j, NT)
        landing = acts.at[core, block_rows(z * 8 + lax.div(t, 2), 16), :]
        return copy(mix_out.at[0, p], landing, a_s.at[1, j], a_r.at[1, j], (d, p))

    def first_scatter():
        peers(lambda j: first_copy(j).start())
        mix_in[0, t] = hid[core, sixteen(t), :]

    def first_mix():
        def came(j):
            arrived(mix_in.at[0, lax.rem(t - j + NT, NT)], a_s.at[0, j], a_r.at[0, j])

        peers(came)
        mix(0, 0, HALF)
        peers(lambda j: first_back(j).start())
        acts[core, block_rows(z * 8 + lax.div(t, 2), 16), :] = mix_out[0, t]

    def first_done():
        def came(j):
            p = lax.rem(t - j + NT, NT)
            landing = acts.at[lax.rem(p, 2), block_rows(z * 8 + lax.div(p, 2), 16), :]
            arrived(landing, a_s.at[1, j], a_r.at[1, j])

        peers(came)

    def last_copy(piece, j):
        group, start, size = PIECES[piece]
        p, cols = lax.rem(t + j, NT), pl.ds(start, size)
        src = rot_grad.at[group, sixteen(p), cols]
        return copy(src, mix_in.at[1, t, :, cols], e_s.at[0, piece, j], e_r.at[0, piece, j], (d, p))

    def last_back(piece, j):
        group, start, size = PIECES[piece]
        p, cols = lax.rem(t + j, NT), pl.ds(start, size)
        landing = grad_hid.at[group, sixteen(t), cols]
        return copy(mix_out.at[1, p, :, cols], landing, e_s.at[1, piece, j], e_r.at[1, piece, j], (d, p))

    def last_scatter(piece):
        group, start, size = PIECES[piece]
        peers_of(group, lambda j: last_copy(piece, j).start())

        @pl.when(core == group)
        def _():
            mix_in[1, t, :, start : start + size] = rot_grad[group, sixteen(t), start : start + size]

    def last_mix(piece):
        group, start, size = PIECES[piece]

        def came(j):
            landing = mix_in.at[1, lax.rem(t - j + NT, NT), :, pl.ds(start, size)]
            arrived(landing, e_s.at[0, piece, j], e_r.at[0, piece, j])

        @pl.when(core == group)
        def _():
            peers(came)
            mix(1, start, size)
            peers(lambda j: last_back(piece, j).start())
            grad_hid[group, sixteen(t), start : start + size] = mix_out[1, t, :, start : start + size]

    def last_done():
        for piece, (group, start, size) in enumerate(PIECES):

            def came(j):
                p = lax.rem(t - j + NT, NT)
                landing = grad_hid.at[group, sixteen(p), pl.ds(start, size)]
                arrived(landing, e_s.at[1, piece, j], e_r.at[1, piece, j])

            peers_of(group, came)

    def drain():
        peers(lambda j: first_copy(j).wait_send())
        peers(lambda j: first_back(j).wait_send())
        for piece, (group, _, _) in enumerate(PIECES):
            peers_of(group, lambda j: last_copy(piece, j).wait_send())

            @pl.when(core == group)
            def _():
                peers(lambda j: last_back(piece, j).wait_send())

    own_rows, across_rows = block_rows(2 * y + xh), block_rows(2 * y + 1 - xh)
    diagonal_copy = copy(grad_ref, grads.at[xl, own_rows, :], gd_s, gd_r, diagonal)

    def grad_own():
        @pl.when(core != xl)
        def _():
            arrived(grads.at[core, own_rows, :], gd_s, gd_r)

        mine = grads.at[core, own_rows, :]
        push(mine, mine, gx_s, gx_r, across)
        for r in (1, 3, 2):
            push(mine, mine, gy_s.at[0, r], gy_r.at[0, r], y_peer[r])
        push(mine, mine, gc_s.at[0, 0], gc_r.at[0, 0], sibling)

    def grad_across():
        piece = grads.at[core, across_rows, :]
        arrived(piece, gx_s, gx_r)
        for r in (1, 3, 2):
            push(piece, piece, gy_s.at[1, r], gy_r.at[1, r], y_peer[r])
        push(piece, piece, gc_s.at[1, 0], gc_r.at[1, 0], sibling)

    def grad_y(f, r):
        source = lax.rem(y - r + 4, 4)
        piece = grads.at[core, block_rows(2 * source + (1 - xh if f else xh)), :]
        arrived(piece, gy_s.at[f, r], gy_r.at[f, r])
        push(piece, piece, gc_s.at[f, r], gc_r.at[f, r], sibling)

    def grad_done():
        for f in range(2):
            for r in range(4):
                source = lax.rem(y - r + 4, 4)
                piece = grads.at[1 - core, block_rows(2 * source + (1 - xh if f else xh)), :]
                arrived(piece, gc_s.at[f, r], gc_r.at[f, r])

    def ag_copy(way, s, group):
        block = zmod(z - s) if way == 0 else zmod(z + s)
        piece = acts.at[group, block_rows(block), pl.ds(0, WIDTHS[group])]
        return (piece, piece, ag_s.at[way, s, group], ag_r.at[way, s, group], z_next[way])

    def ag_step(s):
        for way in range(2):
            for group in range(2):
                if s and (s < 4 or way == group):
                    block = zmod(z - s) if way == 0 else zmod(z + s)
                    piece = acts.at[group, block_rows(block), pl.ds(0, WIDTHS[group])]
                    arrived(piece, ag_s.at[way, s - 1, group], ag_r.at[way, s - 1, group])
                if s < 3 or (s == 3 and way == group):
                    push(*ag_copy(way, s, group))

    def rs_push(way, k, s):
        block = zmod(z + 4 - s) if way == 0 else zmod(z - 4 + s)
        if s == 0:
            piece = back[k].at[block_rows(2 * block + way, 64), :]
            landing = ring[k].at[way, 0, pl.ds(0, 64), :]
        else:
            piece = back[k].at[block_rows(block), :]
            landing = ring[k].at[way, s]
        push(piece, landing, rs_s.at[way, k, s], rs_r.at[way, k, s], z_next[way])

    def rs_arrived(way, k, s):
        landing = ring[k].at[way, s, pl.ds(0, B if s else 64), :]
        arrived(landing, rs_s.at[way, k, s], rs_r.at[way, k, s])

    def product(k, h):
        start, size = CHUNKS[k]
        units = slice(start, start + size)
        for strip in STRIPS_OF[k]:
            for part in (0, 1) if h is None else (h,):
                weight_arrived(strip, part)

        def one(m, carry):
            rows = block_rows(m, 256)
            if h == 1:
                term = back[k][rows, :] if k < RING else back_last[k - RING, rows, :]
                term = term.astype(F32) + dot_t(grads[1 - xl, rows, 512:], w_all[1 - xl, units, 512:])
            else:
                seen = slice(0, 512 if h == 0 else DL)
                term = dot_t(grads[xl, rows, :], w_all[xl, units, :])
                term = term + dot_t(grads[1 - xl, rows, seen], w_all[1 - xl, units, seen])
            if k < RING:
                back[k][rows, :] = term.astype(BF16)
            else:
                back_last[k - RING, rows, :] = term.astype(BF16)
            return carry

        lax.fori_loop(0, ROWS // 256, one, 0)

    def back_total(k, arrivals):
        start, size = CHUNKS[k]
        mine = back[k][block_rows(z), :] if k < RING else back_last[k - RING, block_rows(z), :]
        total = mine.astype(F32)
        for came in arrivals:
            total = total + came.astype(F32)
        total = total.astype(BF16)
        for b in range(size // B):
            group, place = divmod(start // B + b, HALF // B)
            rot_grad[group, :, place * B : (place + 1) * B] = total[:, b * B : (b + 1) * B]

    def back_step(k, s):
        if s == 0:
            product(k, None)
            for way in range(2):
                rs_push(way, k, 0)
        elif s < 4:
            for way in range(2):
                rs_arrived(way, k, s - 1)
                block = zmod(z + 4 - s) if way == 0 else zmod(z - 4 + s)
                if s == 1:
                    rows = block_rows(2 * block + way, 64)
                    came = ring[k][way, 0, :64, :]
                else:
                    rows = block_rows(block)
                    came = ring[k][way, s - 1]
                back[k][rows, :] = (back[k][rows, :].astype(F32) + came.astype(F32)).astype(BF16)
                rs_push(way, k, s)
        else:
            for way in range(2):
                rs_arrived(way, k, 3)
            back_total(k, [ring[k][way, 3] for way in range(2)])

    def direct_step(k, s):
        i = k - RING
        if s == 0:
            product(k, 1)
            for j in (4, 3, 5, 2, 6, 1, 7):
                piece = back_last.at[i, block_rows(zmod(z + j)), :]
                push(piece, direct.at[i, j - 1], ds_s.at[i, j], ds_r.at[i, j], z_peer[j])
        else:
            for j in range(1, NZ):
                arrived(direct.at[i, j - 1], ds_s.at[i, j], ds_r.at[i, j])
            back_total(k, [direct[i, j - 1] for j in range(1, NZ)])

    def out_rows(r):
        return block_rows(lax.rem(y + r, 4), 256)

    def out_product(turn, r):
        late, start, size = TURNS[turn]
        width = 1 - xl if late else xl
        rows, share = out_rows(r), pl.ds(0, size)
        for h in range(2):
            cols = slice(start + h * size, start + (h + 1) * size)
            term = dot(acts[0, rows, :], w_all[width, :HALF, cols])
            term = term + dot(acts[1, rows, : WIDTHS[1]], w_all[width, HALF:, cols])
            cpart[turn, h, rows, :size] = term.astype(BF16)
        landing = crecv.at[turn, rows, share]
        push(cpart.at[turn, 1 - core, rows, share], landing, c_s.at[turn, r], c_r.at[turn, r], sibling)

    def out_core_sum(turn, r):
        size = TURNS[turn][2]
        rows, share = out_rows(r), pl.ds(0, size)
        arrived(crecv.at[turn, rows, share], c_s.at[turn, r], c_r.at[turn, r])
        total = cpart[turn, core, rows, :size].astype(F32) + crecv[turn, rows, :size].astype(F32)
        csum[turn, rows, :size] = total.astype(BF16)
        if r:
            landing = yrecv.at[turn, r - 1, :, share]
            push(csum.at[turn, rows, share], landing, y_s.at[turn, r], y_r.at[turn, r], y_peer[r])

    def out_y_part(turn, side):
        size = TURNS[turn][2]
        total = csum[turn, block_rows(2 * y + side), :size].astype(F32)
        for r in range(3):
            total = total + yrecv[turn, r, block_rows(side), :size].astype(F32)
        return total

    def out_y_sum(turn):
        size = TURNS[turn][2]
        share = pl.ds(0, size)
        for r in range(1, 4):
            arrived(yrecv.at[turn, r - 1, :, share], y_s.at[turn, r], y_r.at[turn, r])
        xsend[turn, :, :size] = out_y_part(turn, 1 - xh).astype(BF16)
        push(xsend.at[turn, :, share], xrecv.at[turn, :, share], x_s.at[turn], x_r.at[turn], across)

    def out_cols(turn, sender):
        _, start, size = TURNS[turn]
        return pl.ds(pl.multiple_of(start + sender * size, 256), size)

    def out_copy(turn):
        device = dev(xl_=1 - xl, c_=xl) if turn else sibling
        share = pl.ds(0, TURNS[turn][2])
        return copy(osend.at[turn, :, share], oacc.at[:, out_cols(turn, core)], o_s.at[turn], o_r.at[turn, core], device)

    def out_place(turn):
        size = TURNS[turn][2]
        arrived(xrecv.at[turn, :, pl.ds(0, size)], x_s.at[turn], x_r.at[turn])
        osend[turn, :, :size] = (out_y_part(turn, xh) + xrecv[turn, :, :size].astype(F32)).astype(BF16)
        if turn == 0:

            @pl.when(core == xl)
            def _():
                oacc[:, out_cols(0, core)] = osend[0]

            @pl.when(core != xl)
            def _():
                out_copy(0).start()
        else:
            out_copy(turn).start()

    def out_done():
        @pl.when(core == xl)
        def _():
            arrived(oacc.at[:, out_cols(0, 1 - core)], o_s.at[0], o_r.at[0, 1 - core])

        @pl.when(core != xl)
        def _():
            for turn in (1, 2):
                for sender in range(2):
                    arrived(oacc.at[:, out_cols(turn, sender)], o_s.at[turn], o_r.at[turn, sender])

    first_scatter()
    weight_push(0, 0)
    fetches[4].wait()

    @pl.when(core != xl)
    def _():
        diagonal_copy.start()

    @pl.when(core == xl)
    def _():
        grads[core, own_rows, :] = grad_ref[...]

    fetches[5].wait()
    for k in range(1, len(STRIPS)):
        dequantize(k)
    fetches[6].wait()
    first_mix()
    grad_own()
    for k, h in ORDER[1:]:
        weight_push(k, h)
    first_done()
    ag_step(0)
    grad_across()
    for r in (1, 3, 2):
        grad_y(0, r)
    ag_step(1)
    for r in (1, 3, 2):
        grad_y(1, r)
    grad_done()

    starts = (0, 2, 4, 6)

    def tick(i):
        for s in (4, 3, 2, 1, 0):
            if i - s in starts:
                back_step(starts.index(i - s), s)

    tick(0)
    ag_step(2)
    tick(1)
    ag_step(3)
    tick(2)
    ag_step(4)
    tick(3)
    out_product(0, 1)
    out_product(0, 2)
    tick(4)
    out_product(0, 3)
    out_product(0, 0)
    out_core_sum(0, 1)
    out_core_sum(0, 2)
    tick(5)
    out_core_sum(0, 3)
    out_core_sum(0, 0)
    tick(6)
    last_scatter(0)
    for k in (4, 5):
        product(k, 0)
    tick(7)
    for r in (1, 2, 3, 0):
        out_product(1, r)
    direct_step(4, 0)
    tick(8)
    for r in (1, 2, 3, 0):
        out_core_sum(1, r)
    direct_step(5, 0)
    out_y_sum(0)
    for r in (1, 2, 3, 0):
        out_product(2, r)
    tick(9)
    for r in (1, 2, 3, 0):
        out_core_sum(2, r)
    last_mix(0)
    tick(10)
    last_scatter(1)
    out_y_sum(1)
    out_place(0)
    direct_step(4, 1)
    direct_step(5, 1)
    last_scatter(2)
    out_place(1)
    out_y_sum(2)
    last_mix(1)
    last_mix(2)
    out_place(2)
    out_done()
    last_done()
    out_ref[...] = oacc[...]
    grad_ref_out[:, :HALF] = grad_hid[0]
    grad_ref_out[:, HALF:] = grad_hid[1, :, : WIDTHS[1]]

    for op in sent:
        op.wait_send()

    @pl.when(core != xl)
    def _():
        diagonal_copy.wait_send()
        out_copy(0).wait_send()

    out_copy(1).wait_send()
    out_copy(2).wait_send()
    drain()


def hadamard():
    index = np.arange(B)
    bits = index[:, None] & index[None, :]
    parity = sum(bits >> s & 1 for s in range(7)) % 2
    return (1 - 2 * parity).astype(np.float32)


def on_device(gate_act, up_act, down_codes, down_scales, grad_out):
    vmem, dma = pltpu.VMEM, pltpu.SemaphoreType.DMA
    whole = pl.BlockSpec(memory_space=pltpu.VMEM)
    layer_output, grad_hidden = pl.pallas_call(
        kernel,
        out_shape=(jax.ShapeDtypeStruct((B, DL), BF16), jax.ShapeDtypeStruct((B, FL), BF16)),
        in_specs=[pl.BlockSpec(memory_space=pl.ANY)] * 6,
        out_specs=(whole, whole),
        scratch_shapes=[
            vmem((B, FL), BF16),
            vmem((B, FL), BF16),
            vmem((FL, DL), BF16),
            vmem((DL // B, FL // B), F32),
            vmem((B, DL), BF16),
            vmem((B, B), BF16),
            vmem((2, FL, DL), BF16),
            vmem((2, B, HALF), BF16),
            vmem((2, NT, 16, HALF), BF16),
            vmem((2, NT, 16, HALF), BF16),
            vmem((2, ROWS, HALF), BF16),
            vmem((2, ROWS, DL), BF16),
            vmem((3, 2, ROWS, 512), BF16),
            vmem((3, ROWS, 512), BF16),
            vmem((3, ROWS, 512), BF16),
            vmem((3, 3, 256, 512), BF16),
            vmem((3, B, 512), BF16),
            vmem((3, B, 512), BF16),
            vmem((3, B, 512), BF16),
            vmem((B, DL), BF16),
            *(vmem((ROWS, size), BF16) for _, size in CHUNKS[:RING]),
            *(vmem((2, 4, B, size), BF16) for _, size in CHUNKS[:RING]),
            vmem((len(CHUNKS) - RING, ROWS, B), BF16),
            vmem((len(CHUNKS) - RING, NZ - 1, B, B), BF16),
            vmem((2, B, HALF), BF16),
            vmem((2, B, HALF), BF16),
            dma((7,)),
            dma((2, len(STRIPS))), dma((2, len(STRIPS))),
            dma((2, NT)), dma((2, NT)),
            dma((2, 3, NT)), dma((2, 3, NT)),
            dma((2, 4, 2)), dma((2, 4, 2)),
            dma, dma,
            dma, dma,
            dma((2, 4)), dma((2, 4)),
            dma((2, 4)), dma((2, 4)),
            dma((3, 4)), dma((3, 4)),
            dma((3, 4)), dma((3, 4)),
            dma((3,)), dma((3,)),
            dma((3,)), dma((3, 2)),
            dma((2, RING, 4)), dma((2, RING, 4)),
            dma((2, NZ)), dma((2, NZ)),
        ],
        compiler_params=pltpu.CompilerParams(
            collective_id=0, has_side_effects=True, vmem_limit_bytes=56 * 1024 * 1024
        ),
    )(gate_act, up_act, down_codes, down_scales.T, grad_out, jnp.asarray(hadamard(), BF16))
    grad_hidden = grad_hidden.astype(F32)
    gate, up = gate_act.astype(F32), up_act.astype(F32)
    sig = jax.nn.sigmoid(gate)
    up_grad = (grad_hidden * (gate * sig)).astype(BF16)
    gate_grad = (grad_hidden * up * sig * (1.0 + gate * (1.0 - sig))).astype(BF16)
    return (layer_output, gate_grad, up_grad)


def solution(mesh):
    return jax.shard_map(
        on_device,
        mesh=mesh,
        in_specs=(
            P("dp", "tensor"),
            P("dp", "tensor"),
            P("tensor", "dp"),
            P("tensor", "dp"),
            P("tensor", "dp"),
        ),
        out_specs=(P("tensor", "dp"), P("dp", "tensor"), P("dp", "tensor")),
        check_vma=False,
    )
```

time: 150 us -> 145 us (0.967)
  Pallas kernels: 145 us -> 140 us
    pallas_call x1, Pallas kernels: 145 us -> 140 us  [on_device(): pl.pallas_call(kernel, out_shape=(jax.ShapeDtypeStruct((B, DL), BF16), ja...]
where the time goes in v3:
time: 145 us
  Pallas kernels  140 us (97%)
  other arithmetic  2.37 us (2%)
  local copies, waits for them, and re-layouts  1.68 us (1%)
    pallas_call x1, Pallas kernels, on_device(): pl.pallas_call(kernel, out_shape=(jax.ShapeDtypeStruct((B, DL), BF16), ja...  140 us

profile of v3, /device:TPU:1, one launch (start us, length us, event | category | flops | bytes accessed | tf_op | source)
XLA Modules:
  0.0 144.6 jit_solution(12300727805327334898)
XLA Ops:
  0.6 0.0 copy-start.1
  0.6 0.0 copy-start
  0.7 139.9 %shard_map.85 = (bf16[128,1024]{1,0:T(8,128)(2,1)}, bf16[128,1664]{1,0:T(8,128)(2,1)}) custom-call(bf16[128,1664]{1,0:T(8,128)(2,1)} %gate_hbm.1, bf16[128,1664]{1,0:T(8,128)(2,1)} %up_hbm.1, bf16[1664,1024]{1,0:T(8,128)(2,1)} %codes_hbm.1, f32[8,13]{1,0:T(8,128)} %bitcast.1, bf16[128,1024]{1,0:T(8,128)(2,1)} %grad_hbm.1, bf16[128,128]{1,0:T(8,128)(2,1)} %constant.4.clone.had_hbm), custom_call_target="tpu_custom_call" | custom-call | tf_op jit(solution)/shard_map/pallas_call | solution.py:585
  140.6 0.0 copy-done.1
  140.6 0.0 copy-done
  140.6 2.4 %fusion.3 = (bf16[128,1664]{1,0:T(8,128)(2,1)}, bf16[128,1664]{1,0:T(8,128)(2,1)}) fusion(bf16[128,1664]{1,0:T(8,128)(2,1)} %get-tuple-element.6, bf16[128,1664]{1,0:T(8,128)(2,1)S(1)} %copy-done, bf16[128,1664]{1,0:T(8,128)(2,1)S(1)} %copy-done.1), kind=kLoop, calls=%fused_computation.8 | loop fusion | flops 3407872 | bytes 2129920 | tf_op jit(solution)/shard_map/convert_element_type | solution.py:640
  142.9 1.7 %copy.10 = bf16[128,1024]{1,0:T(8,128)(2,1)} copy(bf16[128,1024]{1,0:T(8,128)(2,1)} %get-tuple-element.12) | data formatting | bytes 524288
Async XLA Ops:
  0.6 139.9 %copy-start.1 = (bf16[128,1664]{1,0:T(8,128)(2,1)S(1)}, bf16[128,1664]{1,0:T(8,128)(2,1)}, u32[]{:S(2)}) copy-start(bf16[128,1664]{1,0:T(8,128)(2,1)} %up_hbm.1) | copy-start | bytes 1277956
  0.6 139.9 %copy-start = (bf16[128,1664]{1,0:T(8,128)(2,1)S(1)}, bf16[128,1664]{1,0:T(8,128)(2,1)}, u32[]{:S(2)}) copy-start(bf16[128,1664]{1,0:T(8,128)(2,1)} %gate_hbm.1) | copy-start | bytes 1277956

commit v4 on v3

--- a/solution.py
+++ b/solution.py
@@ -300,8 +300,8 @@
         return (piece, piece, ag_s.at[way, s, group], ag_r.at[way, s, group], z_next[way])
 
     def ag_step(s):
-        for way in range(2):
-            for group in range(2):
+        for group in range(2):
+            for way in range(2):
                 if s and (s < 4 or way == group):
                     block = zmod(z - s) if way == 0 else zmod(z + s)
                     piece = acts.at[group, block_rows(block), pl.ds(0, WIDTHS[group])]
@@ -469,7 +469,6 @@
                     arrived(oacc.at[:, out_cols(turn, sender)], o_s.at[turn], o_r.at[turn, sender])
 
     first_scatter()
-    weight_push(0, 0)
     fetches[4].wait()
 
     @pl.when(core != xl)
@@ -480,6 +479,7 @@
     def _():
         grads[core, own_rows, :] = grad_ref[...]
 
+    weight_push(0, 0)
     fetches[5].wait()
     for k in range(1, len(STRIPS)):
         dequantize(k)
@@ -570,6 +570,20 @@
     out_copy(1).wait_send()
     out_copy(2).wait_send()
     drain()
+
+
+def finish(gate_ref, up_ref, grad_ref, sums_ref, out_ref, gate_grad_ref, up_grad_ref):
+    def some_rows(i, carry):
+        rows = block_rows(i, 16)
+        gate, up = gate_ref[rows, :].astype(F32), up_ref[rows, :].astype(F32)
+        grad = grad_ref[rows, :].astype(F32)
+        sig = jax.nn.sigmoid(gate)
+        up_grad_ref[rows, :] = (grad * (gate * sig)).astype(BF16)
+        gate_grad_ref[rows, :] = (grad * up * sig * (1.0 + gate * (1.0 - sig))).astype(BF16)
+        return carry
+
+    lax.fori_loop(0, B // 16, some_rows, 0)
+    out_ref[...] = sums_ref[...]
 
 
 def hadamard():
@@ -634,11 +648,16 @@
             collective_id=0, has_side_effects=True, vmem_limit_bytes=56 * 1024 * 1024
         ),
     )(gate_act, up_act, down_codes, down_scales.T, grad_out, jnp.asarray(hadamard(), BF16))
-    grad_hidden = grad_hidden.astype(F32)
-    gate, up = gate_act.astype(F32), up_act.astype(F32)
-    sig = jax.nn.sigmoid(gate)
-    up_grad = (grad_hidden * (gate * sig)).astype(BF16)
-    gate_grad = (grad_hidden * up * sig * (1.0 + gate * (1.0 - sig))).astype(BF16)
+    layer_output, gate_grad, up_grad = pl.pallas_call(
+        finish,
+        out_shape=(
+            jax.ShapeDtypeStruct((B, DL), BF16),
+            jax.ShapeDtypeStruct((B, FL), BF16),
+            jax.ShapeDtypeStruct((B, FL), BF16),
+        ),
+        in_specs=[whole] * 4,
+        out_specs=(whole,) * 3,
+    )(gate_act, up_act, grad_hidden, layer_output)
     return (layer_output, gate_grad, up_grad)
 
 

time: 145 us -> 143 us (0.986)
  Pallas kernels: 140 us -> 143 us
  other arithmetic: 2.37 us -> 0 us
  local copies, waits for them, and re-layouts: 1.68 us -> 0 us
    pallas_call x0 -> x1, Pallas kernels: none -> 2.87 us  [on_device(): pl.pallas_call(finish, out_shape=(jax.ShapeDtypeStruct((B, DL), BF16), ja...]
    convert_element_type x1 -> x0, other arithmetic: 2.37 us -> none  [on_device(): up_grad = (grad_hidden * (gate * sig)).astype(BF16)]
    unnamed x5 -> x0, local copies, waits for them, and re-layouts: 1.68 us -> none
where the time goes in v4:
time: 143 us
  Pallas kernels  143 us (100%)
    pallas_call x1, Pallas kernels, on_device(): pl.pallas_call(kernel, out_shape=(jax.ShapeDtypeStruct((B, DL), BF16), ja...  140 us
    pallas_call x1, Pallas kernels, on_device(): pl.pallas_call(finish, out_shape=(jax.ShapeDtypeStruct((B, DL), BF16), ja...  2.87 us

profile of v4, /device:TPU:1, one launch (start us, length us, event | category | flops | bytes accessed | tf_op | source)
XLA Modules:
  0.0 143.2 jit_solution(835005554887265650)
XLA Ops:
  0.6 139.7 %shard_map.85 = (bf16[128,1024]{1,0:T(8,128)(2,1)}, bf16[128,1664]{1,0:T(8,128)(2,1)}) custom-call(bf16[128,1664]{1,0:T(8,128)(2,1)} %gate_ref.1, bf16[128,1664]{1,0:T(8,128)(2,1)} %up_ref.1, bf16[1664,1024]{1,0:T(8,128)(2,1)} %codes_hbm.1, f32[8,13]{1,0:T(8,128)} %bitcast.1, bf16[128,1024]{1,0:T(8,128)(2,1)} %grad_hbm.1, bf16[128,128]{1,0:T(8,128)(2,1)} %constant.2.clone.had_hbm), custom_call_target="tpu_custom_call" | custom-call | tf_op jit(solution)/shard_map/pallas_call | solution.py:599
  140.3 2.9 %shard_map.86 = (bf16[128,1024]{1,0:T(8,128)(2,1)}, bf16[128,1664]{1,0:T(8,128)(2,1)}, bf16[128,1664]{1,0:T(8,128)(2,1)}) custom-call(bf16[128,1664]{1,0:T(8,128)(2,1)} %gate_ref.1, bf16[128,1664]{1,0:T(8,128)(2,1)} %up_ref.1, bf16[128,1664]{1,0:T(8,128)(2,1)} %get-tuple-element.5.grad_ref, bf16[128,1024]{1,0:T(8,128)(2,1)} %get-tuple-element.6.sums_ref), custom_call_target="tpu_custom_call" | custom-call | tf_op jit(solution)/shard_map/pallas_call | solution.py:651
